TPU v7x, 32 devices: a whole 2x2x4 slice. The times are simulated.
32 devices in a mesh: groups: 2 (over x), ep: 16 (over z, y, core).
Axes of the slice: x: 2, y: 2, z: 4, core: 2. Of those that a mesh axis runs over, the one named last changes fastest.
Arguments:
- rows_in: bfloat16 [4096, 7168], P(('groups', 'ep')), parts along dimension 0, may hold values from -6 to 6
- expert_ids: int32 [4096, 8], P(('groups', 'ep')), parts along dimension 0, may hold values from 0 to 255, all different within a row; in each aligned block of 128 rows (0 to 127, 128 to 255, ...) at most 8 rows name the same one
- gate_values: float32 [4096, 8], P(('groups', 'ep')), parts along dimension 0, may hold values from 0.2 to 1
- gate_w: bfloat16 [7168, 8192], P(None, 'ep'), may hold values from -0.0625 to 0.0625
- up_w: bfloat16 [7168, 8192], P(None, 'ep'), may hold values from -0.0625 to 0.0625
- down_w: bfloat16 [8192, 7168], P('ep'), may hold values from -0.125 to 0.125
Outputs:
- mixed: bfloat16 [4096, 7168], P(('groups', 'ep')), parts along dimension 0
There are 2 independent parts, one for each index of `groups`. A program takes and returns all parts, laid end to end along the dimension named above; an argument that names none is the same for every part. Nothing has to cross between parts.
Inputs may be any that keep to these rules, and one draw needn't show every extreme that they name: `expert_ids`: each row names 8 different experts. Among the rows of one device no expert is named more than 8 times.
All inputs are finite; a program needn't handle non-finite values.
Results may differ from a plain program's by a relative error of at most 0.0049.
Values may be sent and summed in bfloat16 or wider, within the bound.
A program may use at most 128 MiB of HBM per device.

v0:
```python
import jax
import jax.numpy as jnp
from jax import lax
from jax.sharding import PartitionSpec as P

ETP = 4
CAP = 8


def body(rows_in, expert_ids, gate_values, gate_w, up_w, down_w):
    devices = lax.axis_size("ep")
    row_count, width = rows_in.shape
    window = devices // ETP
    slot_count = window * CAP
    flat = expert_ids.reshape(-1)
    onehot = (flat[:, None] == jnp.arange(window, dtype=jnp.int32)[None, :]).astype(jnp.int32)
    before = jnp.cumsum(onehot, axis=0) - onehot
    place = jnp.sum(before * onehot, axis=1)
    target = jnp.where(flat < window, flat * CAP + place, -1).reshape(expert_ids.shape)
    match = target[:, :, None] == jnp.arange(slot_count, dtype=jnp.int32)[None, None, :]
    picker = jnp.sum(match.astype(jnp.float32), axis=1).astype(jnp.bfloat16)
    weights = jnp.sum(jnp.where(match, gate_values[:, :, None], jnp.float32(0.0)), axis=1)
    buffer = jnp.einsum("rs,rd->sd", picker, rows_in, preferred_element_type=jnp.float32).astype(
        jnp.bfloat16
    )
    buffer = buffer.reshape(window, CAP, width)
    outgoing = jnp.broadcast_to(buffer[:, None], (window, ETP, CAP, width)).reshape(
        devices, CAP, width
    )
    arrived = lax.all_to_all(outgoing, "ep", split_axis=0, concat_axis=0, tiled=True)
    inputs = arrived.reshape(devices * CAP, width)
    gate = jnp.dot(inputs, gate_w, preferred_element_type=jnp.float32)
    upper_proj = jnp.dot(inputs, up_w, preferred_element_type=jnp.float32)
    hidden = (jax.nn.silu(gate) * upper_proj).astype(jnp.bfloat16)
    partial_value = jnp.dot(hidden, down_w, preferred_element_type=jnp.float32).reshape(
        devices, CAP, width
    )
    returned = lax.all_to_all(partial_value, "ep", split_axis=0, concat_axis=0, tiled=True)
    expert_out = jnp.sum(returned.reshape(window, ETP, CAP, width), axis=1)
    mixed = jnp.dot(
        weights,
        expert_out.reshape(slot_count, width),
        precision=lax.Precision.HIGHEST,
        preferred_element_type=jnp.float32,
    )
    return mixed.astype(jnp.bfloat16)


def solution(mesh):
    in_specs = (
        P(("groups", "ep"), None),
        P(("groups", "ep"), None),
        P(("groups", "ep"), None),
        P(None, "ep"),
        P(None, "ep"),
        P("ep", None),
    )
    out_specs = P(("groups", "ep"), None)
    return jax.shard_map(body, mesh=mesh, in_specs=in_specs, out_specs=out_specs, check_vma=False)
```

profile of v0, /device:TPU:0, one launch (start us, length us, event | category | flops | bytes accessed | tf_op | source)
XLA Modules:
  0.0 156.6 jit_solution(6676198074577284137)
XLA Ops:
  0.0 0.0 copy-start
  0.0 0.9 copy.23
  0.9 0.1 eq.42
  1.0 0.1 eq.38
  1.1 1.1 reduce-window.6
  2.3 0.2 slice_reduce_fusion
  2.5 0.2 reduce-window.9
  2.7 0.1 add_bitcast_fusion
  2.8 0.1 reduce_sum.39
  2.9 0.7 add_select_fusion
  3.6 0.7 convert_reduce_fusion
  4.3 0.0 copy-done
  4.4 0.0 copy-start.2
  4.4 0.4 fusion
  4.7 0.2 broadcast_in_dim.30
  4.9 50.2 %all_to_all.10 = bf16[16,8,7168]{2,1,0:T(8,128)(2,1)S(1)} all-to-all(bf16[16,8,7168]{2,1,0:T(8,128)(2,1)S(1)} %bitcast.46), channel_id=1, replica_groups=mesh['groups'=2,'ep'=16] {'ep'}, dimensions={0} | all-to-all | bytes 3670016 | tf_op jit(solution)/shard_map/all_to_all | solution.py:30
  55.1 0.0 copy-start.1
  55.1 1.2 copy-done.1
  56.4 0.0 copy-done.2
  56.4 1.1 fusion.3
  57.5 9.7 %convolution_bitcast_fusion = f32[16,8,7168]{2,1,0:T(8,128)} fusion(bf16[512,7168]{1,0:T(8,128)(2,1)} %param.11, bf16[7168,512]{1,0:T(8,128)(2,1)} %param.10, bf16[16,8,7168]{2,1,0:T(8,128)(2,1)} %copy-done.1, f32[128,512]{1,0:T(8,128)S(1)} %fusion.3), kind=kOutput, calls=%fused_computation | convolution fusion | flops 1879441408 | bytes 20447232 | tf_op jit(solution)/shard_map/dot_general | solution.py:35
  67.2 85.0 %all_to_all.11 = f32[16,8,7168]{2,1,0:T(8,128)S(1)} all-to-all(f32[16,8,7168]{2,1,0:T(8,128)} %convolution_bitcast_fusion), channel_id=1, replica_groups=mesh['groups'=2,'ep'=16] {'ep'}, dimensions={0} | all-to-all | bytes 7340032 | tf_op jit(solution)/shard_map/all_to_all | solution.py:38
  152.2 0.2 bitcast_reduce_fusion
  152.4 4.2 %convolution_convert_fusion = bf16[128,7168]{1,0:T(8,128)(2,1)} fusion(f32[128,32]{0,1:T(8,128)S(1)} %get-tuple-element.6, f32[4,8,7168]{2,1,0:T(8,128)S(1)} %bitcast_reduce_fusion), kind=kOutput, calls=%fused_computation.1 | convolution fusion | flops 353239040 | bytes 2768896 | tf_op jit(solution)/shard_map/dot_general | solution.py:40
  (3 shorter events, 0.1 us)
Async XLA Ops:
  0.0 4.3 %copy-start = (bf16[128,7168]{1,0:T(8,128)(2,1)S(1)}, bf16[128,7168]{1,0:T(8,128)(2,1)}, u32[]{:S(2)}) copy-start(bf16[128,7168]{1,0:T(8,128)(2,1)} %param.6) | copy-start | bytes 5505028
  4.4 52.0 %copy-start.2 = (bf16[7168,512]{1,0:T(8,128)(2,1)S(1)}, bf16[7168,512]{1,0:T(8,128)(2,1)}, u32[]{:S(2)}) copy-start(bf16[7168,512]{1,0:T(8,128)(2,1)} %param.9) | copy-start | bytes 22020100
  55.1 1.2 copy-start.1
where the time goes:
time: 157 us
  blocking collectives  135 us (86%)
  matrix products  15.4 us (10%)
  other arithmetic  3.06 us (2%)
  local copies, waits for them, and re-layouts  2.86 us (2%)
    all_to_all x1, blocking collectives, body(): lax.all_to_all(partial_value, 'ep', split_axis=0, concat_axis=0, tiled=True)  85 us
    all_to_all x1, blocking collectives, body(): lax.all_to_all(outgoing, 'ep', split_axis=0, concat_axis=0, tiled=True)  50.2 us
    dot_general x1, matrix products, body(): jnp.dot(hidden, down_w, preferred_element_type=jnp.float32)  9.7 us
    dot_general x1, matrix products, body(): jnp.dot(weights, expert_out.reshape(slot_count, width), precision=lax.Pre...  4.22 us

commit v1 on v0

v1 whole, which is shorter than its diff:
```python
import functools

import jax
import jax.numpy as jnp
from jax import lax
from jax.experimental import pallas as pl
from jax.experimental.pallas import tpu as pltpu
from jax.sharding import PartitionSpec as P

ETP = 4
CAP = 8
MESH = pl.DeviceIdType.MESH


def flip(number, mask):
    result = number
    bit = 1
    while bit <= mask:
        if mask & bit:
            digit = lax.rem(lax.div(number, jnp.int32(bit)), jnp.int32(2))
            result = result + bit - 2 * bit * digit
        bit *= 2
    return result


def kernel(
    window, chunks,
    ids_ref, gates_ref, rows_hbm, gate_hbm, up_hbm, down_hbm,
    out_ref,
    rows, gate_w, up_w, down_w, block, arrived, inputs, hidden,
    own, core_out, core_in, side_out, side_in, home_out, home_in,
    load_sem, disp_send, disp_recv, core_send, core_recv, side_send, side_recv,
    home_send, home_recv,
):
    width = rows.shape[1]
    row_count = rows.shape[0]
    piece = width // chunks
    slots = window * CAP
    me = lax.axis_index("ep")
    plane = lax.div(me, jnp.int32(ETP))
    within = lax.rem(me, jnp.int32(ETP))
    sibling = plane * ETP + flip(within, 1)
    side = plane * ETP + flip(within, 2)
    partner = [flip(plane, d) * ETP + within for d in range(window)]

    loads = [
        pltpu.make_async_copy(src, dst, load_sem.at[i])
        for i, (src, dst) in enumerate(
            ((rows_hbm, rows), (gate_hbm, gate_w), (up_hbm, up_w), (down_hbm, down_w))
        )
    ]
    loads[0].start()

    barrier = pltpu.get_barrier_semaphore()
    peers = partner[1:] + [sibling, side]
    for peer in peers:
        pl.semaphore_signal(barrier, inc=1, device_id={"ep": peer}, device_id_type=MESH)

    def remote(src, dst, send, recv, target):
        return pltpu.make_async_remote_copy(
            src_ref=src, dst_ref=dst, send_sem=send, recv_sem=recv,
            device_id={"ep": target}, device_id_type=MESH,
        )

    ids = ids_ref[...]
    gates = gates_ref[...]
    named, valued = [], []
    for d in range(window):
        hit = ids == flip(plane, d)
        one = jnp.sum(jnp.where(hit, 1.0, 0.0), axis=0, keepdims=True)
        val = jnp.sum(jnp.where(hit, gates, 0.0), axis=0, keepdims=True)
        named.append(jnp.broadcast_to(one, (CAP, row_count)))
        valued.append(jnp.broadcast_to(val, (CAP, row_count)))
    named = jnp.concatenate(named, axis=0)
    valued = jnp.concatenate(valued, axis=0)
    earlier = lax.broadcasted_iota(jnp.int32, (row_count, row_count), 0) < lax.broadcasted_iota(
        jnp.int32, (row_count, row_count), 1
    )
    rank = jnp.dot(
        named.astype(jnp.bfloat16),
        jnp.where(earlier, 1.0, 0.0).astype(jnp.bfloat16),
        preferred_element_type=jnp.float32,
    )
    place = lax.rem(lax.broadcasted_iota(jnp.int32, (slots, row_count), 0), jnp.int32(CAP))
    chosen = jnp.logical_and(rank == place.astype(jnp.float32), named > 0.5)
    picker = jnp.where(chosen, 1.0, 0.0).astype(jnp.bfloat16)
    weights = jnp.where(chosen, valued, 0.0)
    high = weights.astype(jnp.bfloat16)
    low = (weights - high.astype(jnp.float32)).astype(jnp.bfloat16)
    both = jnp.concatenate([high.astype(jnp.float32), low.astype(jnp.float32)], axis=0)
    both = jnp.transpose(both).astype(jnp.bfloat16)

    loads[0].wait()
    for load in loads[1:]:
        load.start()
    for k in range(chunks):
        cols = pl.ds(k * piece, piece)
        part = jnp.dot(picker, rows[:, cols], preferred_element_type=jnp.float32)
        part = part.reshape(window, CAP, piece).astype(jnp.bfloat16)
        arrived[0, 0, :, cols] = part[0]
        for d in range(1, window):
            block[d, :, cols] = part[d]

    pl.semaphore_wait(barrier, len(peers))
    along, core, across, relay = [None], [], [], []
    for d in range(window):
        if d:
            along.append(
                remote(block.at[d], arrived.at[0, d], disp_send.at[0, d], disp_recv.at[0, d], partner[d])
            )
        core.append(
            remote(arrived.at[0, d], arrived.at[1, d], disp_send.at[1, d], disp_recv.at[1, d], sibling)
        )
        across.append(
            remote(arrived.at[0, d], arrived.at[2, d], disp_send.at[2, d], disp_recv.at[2, d], side)
        )
        relay.append(
            remote(arrived.at[2, d], arrived.at[3, d], disp_send.at[3, d], disp_recv.at[3, d], sibling)
        )
    across[0].start()
    for d in range(1, window):
        along[d].start()
    core[0].start()
    for d in range(1, window):
        along[d].wait_recv()
        across[d].start()
        core[d].start()
        across[d - 1].wait_recv()
        relay[d - 1].start()

    def gather(g):
        values = arrived[g].astype(jnp.float32).reshape(slots, width)
        inputs[g * slots:(g + 1) * slots, :] = values.astype(jnp.bfloat16)

    gather(0)
    for d in range(window):
        core[d].wait_recv()
    gather(1)
    across[window - 1].wait_recv()
    relay[window - 1].start()
    gather(2)
    for d in range(window):
        relay[d].wait_recv()
    gather(3)

    loads[1].wait()
    loads[2].wait()
    units = gate_w.shape[1]
    tile = 256

    @pl.loop(0, units // tile)
    def _(n):
        cols = pl.ds(pl.multiple_of(n * tile, tile), tile)
        g = jnp.dot(inputs[...], gate_w[:, cols], preferred_element_type=jnp.float32)
        u = jnp.dot(inputs[...], up_w[:, cols], preferred_element_type=jnp.float32)
        hidden[:, cols] = (g / (1.0 + jnp.exp(-g)) * u).astype(jnp.bfloat16)

    loads[3].wait()
    to_core = [
        remote(core_out.at[k], core_in.at[k], core_send.at[k], core_recv.at[k], sibling)
        for k in range(chunks)
    ]
    to_side = [
        remote(side_out.at[k], side_in.at[k], side_send.at[k], side_recv.at[k], side)
        for k in range(chunks)
    ]
    to_home = [
        [
            remote(home_out.at[k, d], home_in.at[k, d], home_send.at[k, d], home_recv.at[k, d], partner[d])
            for d in range(1, window)
        ]
        for k in range(chunks)
    ]

    def pair_sum(k):
        to_core[k].wait_recv()
        side_out[k] = (own[k, slots:, :] + core_in[k, slots:, :].astype(jnp.float32)).astype(jnp.bfloat16)
        to_side[k].start()
        own[k, :slots, :] = own[k, :slots, :] + core_in[k, :slots, :].astype(jnp.float32)

    def full_sum(k):
        to_side[k].wait_recv()
        total = own[k, :slots, :] + side_in[k].astype(jnp.float32)
        total = total.reshape(window, CAP, piece).astype(jnp.bfloat16)
        home_in[k, 0] = total[0]
        for d in range(1, window):
            home_out[k, d] = total[d]
        for copy in to_home[k]:
            copy.start()

    def mix(k):
        for copy in to_home[k]:
            copy.wait_recv()
        values = home_in[k].astype(jnp.float32).reshape(slots, piece)
        values = jnp.concatenate([values, values], axis=0).astype(jnp.bfloat16)
        out_ref[:, k * piece:(k + 1) * piece] = jnp.dot(
            both, values, preferred_element_type=jnp.float32
        ).astype(jnp.bfloat16)

    for k in range(chunks):
        part = jnp.dot(
            hidden[...], down_w[:, k * piece:(k + 1) * piece], preferred_element_type=jnp.float32
        )
        core_out[k, :slots, :] = part[slots:2 * slots].astype(jnp.bfloat16)
        core_out[k, slots:, :] = part[3 * slots:].astype(jnp.bfloat16)
        to_core[k].start()
        own[k, :slots, :] = part[:slots]
        own[k, slots:, :] = part[2 * slots:3 * slots]
        if k >= 1:
            pair_sum(k - 1)
    pair_sum(chunks - 1)
    for k in range(chunks):
        full_sum(k)
        if k >= 2:
            mix(k - 2)
    for k in range(max(chunks - 2, 0), chunks):
        mix(k)

    for copy in along[1:] + core + across + relay + to_core + to_side:
        copy.wait_send()
    for k in range(chunks):
        for copy in to_home[k]:
            copy.wait_send()


def body(rows_in, expert_ids, gate_values, gate_w, up_w, down_w):
    devices = lax.axis_size("ep")
    row_count, width = rows_in.shape
    units = gate_w.shape[1]
    window = devices // ETP
    slots = window * CAP
    chunks = 7
    piece = width // chunks
    bf16, f32 = jnp.bfloat16, jnp.float32
    dma = pltpu.SemaphoreType.DMA
    any_spec = pl.BlockSpec(memory_space=pl.ANY)
    vmem_spec = pl.BlockSpec(memory_space=pltpu.VMEM)
    return pl.pallas_call(
        functools.partial(kernel, window, chunks),
        out_shape=jax.ShapeDtypeStruct((row_count, width), bf16),
        in_specs=[vmem_spec, vmem_spec, any_spec, any_spec, any_spec, any_spec],
        out_specs=vmem_spec,
        scratch_shapes=[
            pltpu.VMEM((row_count, width), bf16),
            pltpu.VMEM((width, units), bf16),
            pltpu.VMEM((width, units), bf16),
            pltpu.VMEM((units, width), bf16),
            pltpu.VMEM((window, CAP, width), bf16),
            pltpu.VMEM((ETP, window, CAP, width), bf16),
            pltpu.VMEM((ETP * slots, width), bf16),
            pltpu.VMEM((ETP * slots, units), bf16),
            pltpu.VMEM((chunks, 2 * slots, piece), f32),
            pltpu.VMEM((chunks, 2 * slots, piece), bf16),
            pltpu.VMEM((chunks, 2 * slots, piece), bf16),
            pltpu.VMEM((chunks, slots, piece), bf16),
            pltpu.VMEM((chunks, slots, piece), bf16),
            pltpu.VMEM((chunks, window, CAP, piece), bf16),
            pltpu.VMEM((chunks, window, CAP, piece), bf16),
            dma((4,)),
            dma((4, window)),
            dma((4, window)),
            dma((chunks,)),
            dma((chunks,)),
            dma((chunks,)),
            dma((chunks,)),
            dma((chunks, window)),
            dma((chunks, window)),
        ],
        compiler_params=pltpu.CompilerParams(
            collective_id=0, has_side_effects=True, vmem_limit_bytes=56 * 1024 * 1024
        ),
    )(expert_ids.T, gate_values.T, rows_in, gate_w, up_w, down_w)


def solution(mesh):
    in_specs = (
        P(("groups", "ep"), None),
        P(("groups", "ep"), None),
        P(("groups", "ep"), None),
        P(None, "ep"),
        P(None, "ep"),
        P("ep", None),
    )
    out_specs = P(("groups", "ep"), None)
    return jax.shard_map(body, mesh=mesh, in_specs=in_specs, out_specs=out_specs, check_vma=False)
```

time: 157 us -> 48 us (0.31)
  blocking collectives: 135 us -> 0 us
  Pallas kernels: 0 us -> 45 us
  matrix products: 15.4 us -> 0 us
  other arithmetic: 3.06 us -> 0 us
    all_to_all x2 -> x0, blocking collectives: 135 us -> none  [the longest x1 85 us: body(): lax.all_to_all(partial_value, 'ep', split_axis=0, concat_axis=0, tiled=True)]
    pallas_call x0 -> x1, Pallas kernels: none -> 45 us  [body(): pl.pallas_call(functools.partial(kernel, window, chunks), out_shape=jax.S...]
    dot_general x4 -> x0, matrix products: 15.4 us -> none  [the longest x1 9.7 us: body(): jnp.dot(hidden, down_w, preferred_element_type=jnp.float32)]
where the time goes in v1:
time: 48 us; the launch traced here: 47.8 us
  Pallas kernels  45 us (94%)
  local copies, waits for them, and re-layouts  2.85 us (6%)
    pallas_call x1, Pallas kernels, body(): pl.pallas_call(functools.partial(kernel, window, chunks), out_shape=jax.S...  45 us
    unnamed x1, local copies, waits for them, and re-layouts  2.85 us

profile of v1, /device:TPU:0, one launch (start us, length us, event | category | flops | bytes accessed | tf_op | source)
XLA Modules:
  0.0 47.8 jit_solution(17162103064216567697)
XLA Ops:
  0.0 45.0 %shard_map.64 = bf16[128,7168]{1,0:T(8,128)(2,1)} custom-call(s32[8,128]{1,0:T(8,128)} %bitcast.2, f32[8,128]{1,0:T(8,128)} %bitcast.3, bf16[128,7168]{1,0:T(8,128)(2,1)} %rows_hbm.1, bf16[7168,512]{1,0:T(8,128)(2,1)} %gate_hbm.1, bf16[7168,512]{1,0:T(8,128)(2,1)} %up_hbm.1, bf16[512,7168]{1,0:T(8,128)(2,1)} %down_hbm.1), custom_call_target="tpu_custom_call" | custom-call | tf_op jit(solution)/shard_map/pallas_call | solution.py:238
  45.0 2.8 %copy.8 = bf16[128,7168]{1,0:T(8,128)(2,1)} copy(bf16[128,7168]{1,0:T(8,128)(2,1)} %shard_map.64) | data formatting | bytes 3670016

commit v2 on v1

--- a/solution.py
+++ b/solution.py
@@ -24,10 +24,10 @@
 
 
 def kernel(
-    window, chunks,
+    window, chunks, halves,
     ids_ref, gates_ref, rows_hbm, gate_hbm, up_hbm, down_hbm,
-    out_ref,
-    rows, gate_w, up_w, down_w, block, arrived, inputs, hidden,
+    mix_ref, out_ref,
+    rows, gate_w, up_w, down_w, block, arrived, inputs, gate_sum, up_sum, hidden,
     own, core_out, core_in, side_out, side_in, home_out, home_in,
     load_sem, disp_send, disp_recv, core_send, core_recv, side_send, side_recv,
     home_send, home_recv,
@@ -88,72 +88,95 @@
     high = weights.astype(jnp.bfloat16)
     low = (weights - high.astype(jnp.float32)).astype(jnp.bfloat16)
     both = jnp.concatenate([high.astype(jnp.float32), low.astype(jnp.float32)], axis=0)
-    both = jnp.transpose(both).astype(jnp.bfloat16)
+    mix_ref[...] = jnp.transpose(both).astype(jnp.bfloat16)
+
+    half = width // halves
+    along, core, across, relay = [], [], [], []
+    for h in range(halves):
+        for d in range(window):
+            n = h * window + d
+            along.append(
+                remote(block.at[h, d], arrived.at[h, 0, d], disp_send.at[0, n], disp_recv.at[0, n], partner[d])
+                if d else None
+            )
+            core.append(
+                remote(arrived.at[h, 0, d], arrived.at[h, 1, d], disp_send.at[1, n], disp_recv.at[1, n], sibling)
+            )
+            across.append(
+                remote(arrived.at[h, 0, d], arrived.at[h, 2, d], disp_send.at[2, n], disp_recv.at[2, n], side)
+            )
+            relay.append(
+                remote(arrived.at[h, 2, d], arrived.at[h, 3, d], disp_send.at[3, n], disp_recv.at[3, n], sibling)
+            )
 
     loads[0].wait()
+    for h in range(halves):
+        part = jnp.dot(
+            picker, rows[:, h * half:(h + 1) * half], preferred_element_type=jnp.float32
+        )
+        part = part.reshape(window, CAP, half).astype(jnp.bfloat16)
+        arrived[h, 0, 0] = part[0]
+        for d in range(1, window):
+            block[h, d] = part[d]
+        if h == 0:
+            pl.semaphore_wait(barrier, len(peers))
+        across[h * window].start()
+        for d in range(1, window):
+            along[h * window + d].start()
+        core[h * window].start()
     for load in loads[1:]:
         load.start()
-    for k in range(chunks):
-        cols = pl.ds(k * piece, piece)
-        part = jnp.dot(picker, rows[:, cols], preferred_element_type=jnp.float32)
-        part = part.reshape(window, CAP, piece).astype(jnp.bfloat16)
-        arrived[0, 0, :, cols] = part[0]
+
+    passed = 0
+    for h in range(halves):
         for d in range(1, window):
-            block[d, :, cols] = part[d]
-
-    pl.semaphore_wait(barrier, len(peers))
-    along, core, across, relay = [None], [], [], []
-    for d in range(window):
-        if d:
-            along.append(
-                remote(block.at[d], arrived.at[0, d], disp_send.at[0, d], disp_recv.at[0, d], partner[d])
-            )
-        core.append(
-            remote(arrived.at[0, d], arrived.at[1, d], disp_send.at[1, d], disp_recv.at[1, d], sibling)
-        )
-        across.append(
-            remote(arrived.at[0, d], arrived.at[2, d], disp_send.at[2, d], disp_recv.at[2, d], side)
-        )
-        relay.append(
-            remote(arrived.at[2, d], arrived.at[3, d], disp_send.at[3, d], disp_recv.at[3, d], sibling)
-        )
-    across[0].start()
-    for d in range(1, window):
-        along[d].start()
-    core[0].start()
-    for d in range(1, window):
-        along[d].wait_recv()
-        across[d].start()
-        core[d].start()
-        across[d - 1].wait_recv()
-        relay[d - 1].start()
-
-    def gather(g):
-        values = arrived[g].astype(jnp.float32).reshape(slots, width)
-        inputs[g * slots:(g + 1) * slots, :] = values.astype(jnp.bfloat16)
-
-    gather(0)
-    for d in range(window):
-        core[d].wait_recv()
-    gather(1)
-    across[window - 1].wait_recv()
-    relay[window - 1].start()
-    gather(2)
-    for d in range(window):
-        relay[d].wait_recv()
-    gather(3)
-
-    loads[1].wait()
-    loads[2].wait()
+            n = h * window + d
+            along[n].wait_recv()
+            across[n].start()
+            core[n].start()
+            while passed < n and (passed + 1 < n or d > 1):
+                across[passed].wait_recv()
+                relay[passed].start()
+                passed += 1
+
+    def gather(h, g):
+        values = arrived[h, g].astype(jnp.float32).reshape(slots, half)
+        inputs[h, g * slots:(g + 1) * slots, :] = values.astype(jnp.bfloat16)
+
     units = gate_w.shape[1]
     tile = 256
-
-    @pl.loop(0, units // tile)
-    def _(n):
-        cols = pl.ds(pl.multiple_of(n * tile, tile), tile)
-        g = jnp.dot(inputs[...], gate_w[:, cols], preferred_element_type=jnp.float32)
-        u = jnp.dot(inputs[...], up_w[:, cols], preferred_element_type=jnp.float32)
-        hidden[:, cols] = (g / (1.0 + jnp.exp(-g)) * u).astype(jnp.bfloat16)
+    for h in range(halves):
+        last = h == halves - 1
+        gather(h, 0)
+        for d in range(window):
+            core[h * window + d].wait_recv()
+        gather(h, 1)
+        while passed < (h + 1) * window:
+            across[passed].wait_recv()
+            relay[passed].start()
+            passed += 1
+        gather(h, 2)
+        for d in range(window):
+            relay[h * window + d].wait_recv()
+        gather(h, 3)
+        if h == 0:
+            loads[1].wait()
+            loads[2].wait()
+
+        @pl.loop(0, units // tile)
+        def _(n):
+            cols = pl.ds(pl.multiple_of(n * tile, tile), tile)
+            deep = pl.ds(h * half, half)
+            g = jnp.dot(inputs[h], gate_w[deep, cols], preferred_element_type=jnp.float32)
+            u = jnp.dot(inputs[h], up_w[deep, cols], preferred_element_type=jnp.float32)
+            if h > 0:
+                g = g + gate_sum[:, cols]
+                u = u + up_sum[:, cols]
+            if last:
+                hidden[:, cols] = (g / (1.0 + jnp.exp(-g)) * u).astype(jnp.bfloat16)
+            else:
+                gate_sum[:, cols] = g
+                up_sum[:, cols] = u
 
     loads[3].wait()
     to_core = [
@@ -192,10 +215,9 @@
         for copy in to_home[k]:
             copy.wait_recv()
         values = home_in[k].astype(jnp.float32).reshape(slots, piece)
-        values = jnp.concatenate([values, values], axis=0).astype(jnp.bfloat16)
-        out_ref[:, k * piece:(k + 1) * piece] = jnp.dot(
-            both, values, preferred_element_type=jnp.float32
-        ).astype(jnp.bfloat16)
+        values = values.astype(jnp.bfloat16)
+        out_ref[:slots, k * piece:(k + 1) * piece] = values
+        out_ref[slots:, k * piece:(k + 1) * piece] = values
 
     for k in range(chunks):
         part = jnp.dot(
@@ -211,12 +233,11 @@
     pair_sum(chunks - 1)
     for k in range(chunks):
         full_sum(k)
-        if k >= 2:
-            mix(k - 2)
-    for k in range(max(chunks - 2, 0), chunks):
+    for k in range(chunks):
         mix(k)
 
-    for copy in along[1:] + core + across + relay + to_core + to_side:
+    sent = [copy for copy in along if copy is not None]
+    for copy in sent + core + across + relay + to_core + to_side:
         copy.wait_send()
     for k in range(chunks):
         for copy in to_home[k]:
@@ -230,24 +251,31 @@
     window = devices // ETP
     slots = window * CAP
     chunks = 7
+    halves = 2
+    half = width // halves
     piece = width // chunks
     bf16, f32 = jnp.bfloat16, jnp.float32
     dma = pltpu.SemaphoreType.DMA
     any_spec = pl.BlockSpec(memory_space=pl.ANY)
     vmem_spec = pl.BlockSpec(memory_space=pltpu.VMEM)
-    return pl.pallas_call(
-        functools.partial(kernel, window, chunks),
-        out_shape=jax.ShapeDtypeStruct((row_count, width), bf16),
+    mix, values = pl.pallas_call(
+        functools.partial(kernel, window, chunks, halves),
+        out_shape=(
+            jax.ShapeDtypeStruct((row_count, 2 * slots), bf16),
+            jax.ShapeDtypeStruct((2 * slots, width), bf16),
+        ),
         in_specs=[vmem_spec, vmem_spec, any_spec, any_spec, any_spec, any_spec],
-        out_specs=vmem_spec,
+        out_specs=(vmem_spec, vmem_spec),
         scratch_shapes=[
             pltpu.VMEM((row_count, width), bf16),
             pltpu.VMEM((width, units), bf16),
             pltpu.VMEM((width, units), bf16),
             pltpu.VMEM((units, width), bf16),
-            pltpu.VMEM((window, CAP, width), bf16),
-            pltpu.VMEM((ETP, window, CAP, width), bf16),
-            pltpu.VMEM((ETP * slots, width), bf16),
+            pltpu.VMEM((halves, window, CAP, half), bf16),
+            pltpu.VMEM((halves, ETP, window, CAP, half), bf16),
+            pltpu.VMEM((halves, ETP * slots, half), bf16),
+            pltpu.VMEM((ETP * slots, units), f32),
+            pltpu.VMEM((ETP * slots, units), f32),
             pltpu.VMEM((ETP * slots, units), bf16),
             pltpu.VMEM((chunks, 2 * slots, piece), f32),
             pltpu.VMEM((chunks, 2 * slots, piece), bf16),
@@ -257,8 +285,8 @@
             pltpu.VMEM((chunks, window, CAP, piece), bf16),
             pltpu.VMEM((chunks, window, CAP, piece), bf16),
             dma((4,)),
-            dma((4, window)),
-            dma((4, window)),
+            dma((4, halves * window)),
+            dma((4, halves * window)),
             dma((chunks,)),
             dma((chunks,)),
             dma((chunks,)),
@@ -270,6 +298,7 @@
             collective_id=0, has_side_effects=True, vmem_limit_bytes=56 * 1024 * 1024
         ),
     )(expert_ids.T, gate_values.T, rows_in, gate_w, up_w, down_w)
+    return jnp.dot(mix, values, preferred_element_type=f32).astype(bf16)
 
 
 def solution(mesh):

time: 48 us -> 48.2 us (level)
  matrix products: 0 us -> 3.05 us
  local copies, waits for them, and re-layouts: 2.85 us -> 0 us
    dot_general x0 -> x1, matrix products: none -> 3.05 us  [body(): return jnp.dot(mix, values, preferred_element_type=f32).astype(bf16)]
    unnamed x1 -> x0, local copies, waits for them, and re-layouts: 2.85 us -> none
where the time goes in v2:
time: 48.2 us; the launch traced here: 48 us
  Pallas kernels  44.9 us (93%)
  matrix products  3.05 us (6%)
    pallas_call x1, Pallas kernels, body(): pl.pallas_call(functools.partial(kernel, window, chunks, halves), out_sha...  44.9 us
    dot_general x1, matrix products, body(): return jnp.dot(mix, values, preferred_element_type=f32).astype(bf16)  3.05 us

profile of v2, /device:TPU:0, one launch (start us, length us, event | category | flops | bytes accessed | tf_op | source)
XLA Modules:
  0.0 48.0 jit_solution(6143019624939195508)
XLA Ops:
  0.0 44.9 %shard_map.64 = (bf16[128,64]{1,0:T(8,128)(2,1)}, bf16[64,7168]{1,0:T(8,128)(2,1)}) custom-call(s32[8,128]{1,0:T(8,128)} %bitcast.4, f32[8,128]{1,0:T(8,128)} %bitcast.5, bf16[128,7168]{1,0:T(8,128)(2,1)} %rows_hbm.1, bf16[7168,512]{1,0:T(8,128)(2,1)} %gate_hbm.1, bf16[7168,512]{1,0:T(8,128)(2,1)} %up_hbm.1, bf16[512,7168]{1,0:T(8,128)(2,1)} %down_hbm.1), custom_call_target="tpu_custom_call" | custom-call | tf_op jit(solution)/shard_map/pallas_call | solution.py:261
  44.9 3.0 %convolution_convert_fusion = bf16[128,7168]{1,0:T(8,128)(2,1)} fusion(bf16[128,64]{1,0:T(8,128)(2,1)} %get-tuple-element.7, bf16[64,7168]{1,0:T(8,128)(2,1)} %get-tuple-element.8), kind=kOutput, calls=%fused_computation | convolution fusion | flops 118358016 | bytes 2768896 | tf_op jit(solution)/shard_map/dot_general | solution.py:301

commit v3 on v1

--- a/solution.py
+++ b/solution.py
@@ -229,7 +229,7 @@
     units = gate_w.shape[1]
     window = devices // ETP
     slots = window * CAP
-    chunks = 7
+    chunks = 4
     piece = width // chunks
     bf16, f32 = jnp.bfloat16, jnp.float32
     dma = pltpu.SemaphoreType.DMA

time: 48 us -> 47.1 us (0.981)
  Pallas kernels: 45 us -> 44.1 us
    pallas_call x1, Pallas kernels: 45 us -> 44.1 us  [body(): pl.pallas_call(functools.partial(kernel, window, chunks), out_shape=jax.S...]
where the time goes in v3:
time: 47.1 us; the launch traced here: 46.9 us
  Pallas kernels  44.1 us (94%)
  local copies, waits for them, and re-layouts  2.85 us (6%)
    pallas_call x1, Pallas kernels, body(): pl.pallas_call(functools.partial(kernel, window, chunks), out_shape=jax.S...  44.1 us
    unnamed x1, local copies, waits for them, and re-layouts  2.85 us

profile of v3, /device:TPU:0, one launch (start us, length us, event | category | flops | bytes accessed | tf_op | source)
XLA Modules:
  0.0 46.9 jit_solution(11892268463329284258)
XLA Ops:
  0.0 44.1 %shard_map.64 = bf16[128,7168]{1,0:T(8,128)(2,1)} custom-call(s32[8,128]{1,0:T(8,128)} %bitcast.2, f32[8,128]{1,0:T(8,128)} %bitcast.3, bf16[128,7168]{1,0:T(8,128)(2,1)} %rows_hbm.1, bf16[7168,512]{1,0:T(8,128)(2,1)} %gate_hbm.1, bf16[7168,512]{1,0:T(8,128)(2,1)} %up_hbm.1, bf16[512,7168]{1,0:T(8,128)(2,1)} %down_hbm.1), custom_call_target="tpu_custom_call" | custom-call | tf_op jit(solution)/shard_map/pallas_call | solution.py:238
  44.1 2.8 %copy.8 = bf16[128,7168]{1,0:T(8,128)(2,1)} copy(bf16[128,7168]{1,0:T(8,128)(2,1)} %shard_map.64) | data formatting | bytes 3670016

commit v4 on v3

--- a/solution.py
+++ b/solution.py
@@ -26,11 +26,11 @@
 def kernel(
     window, chunks,
     ids_ref, gates_ref, rows_hbm, gate_hbm, up_hbm, down_hbm,
-    out_ref,
-    rows, gate_w, up_w, down_w, block, arrived, inputs, hidden,
+    out_hbm,
+    out, rows, gate_w, up_w, down_w, block, arrived, inputs, hidden,
     own, core_out, core_in, side_out, side_in, home_out, home_in,
     load_sem, disp_send, disp_recv, core_send, core_recv, side_send, side_recv,
-    home_send, home_recv,
+    home_send, home_recv, store_sem,
 ):
     width = rows.shape[1]
     row_count = rows.shape[0]
@@ -188,14 +188,20 @@
         for copy in to_home[k]:
             copy.start()
 
+    stores = [
+        pltpu.make_async_copy(out.at[k], out_hbm.at[:, pl.ds(k * piece, piece)], store_sem.at[k])
+        for k in range(chunks)
+    ]
+
     def mix(k):
         for copy in to_home[k]:
             copy.wait_recv()
         values = home_in[k].astype(jnp.float32).reshape(slots, piece)
         values = jnp.concatenate([values, values], axis=0).astype(jnp.bfloat16)
-        out_ref[:, k * piece:(k + 1) * piece] = jnp.dot(
+        out[k] = jnp.dot(
             both, values, preferred_element_type=jnp.float32
         ).astype(jnp.bfloat16)
+        stores[k].start()
 
     for k in range(chunks):
         part = jnp.dot(
@@ -221,6 +227,7 @@
     for k in range(chunks):
         for copy in to_home[k]:
             copy.wait_send()
+        stores[k].wait()
 
 
 def body(rows_in, expert_ids, gate_values, gate_w, up_w, down_w):
@@ -239,8 +246,9 @@
         functools.partial(kernel, window, chunks),
         out_shape=jax.ShapeDtypeStruct((row_count, width), bf16),
         in_specs=[vmem_spec, vmem_spec, any_spec, any_spec, any_spec, any_spec],
-        out_specs=vmem_spec,
+        out_specs=any_spec,
         scratch_shapes=[
+            pltpu.VMEM((chunks, row_count, piece), bf16),
             pltpu.VMEM((row_count, width), bf16),
             pltpu.VMEM((width, units), bf16),
             pltpu.VMEM((width, units), bf16),
@@ -265,6 +273,7 @@
             dma((chunks,)),
             dma((chunks, window)),
             dma((chunks, window)),
+            dma((chunks,)),
         ],
         compiler_params=pltpu.CompilerParams(
             collective_id=0, has_side_effects=True, vmem_limit_bytes=56 * 1024 * 1024

time: 47.1 us -> 46.7 us (level)
  Pallas kernels: 44.1 us -> 43.6 us
where the time goes in v4:
time: 46.7 us; the launch traced here: 46.5 us
  Pallas kernels  43.6 us (93%)
  local copies, waits for them, and re-layouts  2.85 us (6%)
    pallas_call x1, Pallas kernels, body(): pl.pallas_call(functools.partial(kernel, window, chunks), out_shape=jax.S...  43.6 us
    unnamed x1, local copies, waits for them, and re-layouts  2.85 us

profile of v4, /device:TPU:0, one launch (start us, length us, event | category | flops | bytes accessed | tf_op | source)
XLA Modules:
  0.0 46.5 jit_solution(13150217341576828965)
XLA Ops:
  0.0 43.6 %shard_map.64 = bf16[128,7168]{1,0:T(8,128)(2,1)} custom-call(s32[8,128]{1,0:T(8,128)} %bitcast.2, f32[8,128]{1,0:T(8,128)} %bitcast.3, bf16[128,7168]{1,0:T(8,128)(2,1)} %rows_hbm.1, bf16[7168,512]{1,0:T(8,128)(2,1)} %gate_hbm.1, bf16[7168,512]{1,0:T(8,128)(2,1)} %up_hbm.1, bf16[512,7168]{1,0:T(8,128)(2,1)} %down_hbm.1), custom_call_target="tpu_custom_call" | custom-call | tf_op jit(solution)/shard_map/pallas_call | solution.py:245
  43.6 2.8 %copy.8 = bf16[128,7168]{1,0:T(8,128)(2,1)} copy(bf16[128,7168]{1,0:T(8,128)(2,1)} %shard_map.64) | data formatting | bytes 3670016
